TPU v7x, 128 devices: a whole 4x4x4 slice. The times are simulated.
128 devices in a mesh: dp: 4 (over y), expert: 32 (over x, z, core).
Axes of the slice: x: 4, y: 4, z: 4, core: 2. Of those that a mesh axis runs over, the one named last changes fastest.
Arguments:
- tokens: bfloat16 [16384, 2048], P(('dp', 'expert')), may hold values from -6 to 6
- out_grad: bfloat16 [16384, 2048], P(('dp', 'expert')), may hold values from -3 to 3
- expert_ids: int32 [16384, 4], P(('dp', 'expert')), may hold values from 0 to 127, all different within a row; in each aligned block of 128 rows (0 to 127, 128 to 255, ...) at most 6 rows name the same one
- route_weight: bfloat16 [16384, 4], P(('dp', 'expert')), may hold values from 0.049804688 to 1
- up_weight: bfloat16 [128, 2048, 1536], P(('dp', 'expert')), may hold values from -0.125 to 0.125
- down_weight: bfloat16 [128, 768, 2048], P(('dp', 'expert')), may hold values from -0.21875 to 0.21875
Outputs:
- token_grad: bfloat16 [16384, 2048], P(('dp', 'expert'))
- route_grad: bfloat16 [16384, 4], P(('dp', 'expert'))
- up_grad: bfloat16 [128, 2048, 1536], P(('dp', 'expert'))
- down_grad: bfloat16 [128, 768, 2048], P(('dp', 'expert'))
Inputs may be any that keep to these rules, and one draw needn't show every extreme that they name: `expert_ids`: each row names 4 different experts. In the rows of one device no expert is named more than 6 times, and in every draw some device names some expert exactly 6 times.
All inputs are finite; a program needn't handle non-finite values.
Results may differ from a plain program's by a relative error of at most 0.0065.
Values may be sent and summed in bfloat16 or wider, within the bound.
No kernel may reach another device: no remote copies, remote signals or barrier semaphores. Data moves between devices by JAX's collectives and lax.ppermute only.
A program may use at most 128 MiB of HBM per device.

v0:
```python
import jax
import jax.numpy as jnp
from jax import lax
from jax.sharding import PartitionSpec as P


def silu_parts(gate_pre):
    sigma = jax.nn.sigmoid(gate_pre)
    return (gate_pre * sigma, sigma * (1.0 + gate_pre * (1.0 - sigma)))


def local(tokens, out_grad, expert_ids, route_weight, up_weight, down_weight):
    dp_size = lax.axis_size("dp")
    ep_size = lax.axis_size("expert")
    devices = dp_size * ep_size
    local_experts = up_weight.shape[0]
    model_width = tokens.shape[1]
    hidden_units = down_weight.shape[1]
    all_experts = devices * local_experts
    tok_rows, top_k = expert_ids.shape
    capacity = 3 * tok_rows * top_k // (2 * all_experts)
    slot_count = all_experts * capacity
    flat_ids = expert_ids.reshape(-1)
    onehot = (flat_ids[:, None] == jnp.arange(all_experts, dtype=jnp.int32)[None, :]).astype(
        jnp.int32
    )
    position = jnp.sum((jnp.cumsum(onehot, axis=0) - 1) * onehot, axis=1)
    target = flat_ids * capacity + position
    placed = (target[:, None] == jnp.arange(slot_count, dtype=jnp.int32)[None, :]).astype(
        jnp.bfloat16
    )
    dispatch = jnp.sum(placed.reshape(tok_rows, top_k, slot_count), axis=1)
    tok_send = jnp.einsum("ts,td->sd", dispatch, tokens, preferred_element_type=jnp.float32).astype(
        jnp.bfloat16
    )
    grad_send = jnp.einsum(
        "ts,td->sd", dispatch, out_grad, preferred_element_type=jnp.float32
    ).astype(jnp.bfloat16)
    weight_send = jnp.dot(
        route_weight.reshape(-1), placed, preferred_element_type=jnp.float32
    ).astype(jnp.bfloat16)
    tok_recv, grad_recv, weight_recv = (
        lax.all_to_all(
            tok_send.reshape(devices, local_experts, capacity, model_width),
            ("dp", "expert"),
            split_axis=0,
            concat_axis=0,
            tiled=True,
        ),
        lax.all_to_all(
            grad_send.reshape(devices, local_experts, capacity, model_width),
            ("dp", "expert"),
            split_axis=0,
            concat_axis=0,
            tiled=True,
        ),
        lax.all_to_all(
            weight_send.reshape(devices, local_experts, capacity),
            ("dp", "expert"),
            split_axis=0,
            concat_axis=0,
            tiled=True,
        ),
    )
    scaled = (weight_recv.astype(jnp.float32)[..., None] * grad_recv.astype(jnp.float32)).astype(
        jnp.bfloat16
    )
    pre_act = jnp.einsum("sjcd,jdf->sjcf", tok_recv, up_weight, preferred_element_type=jnp.float32)
    gate_pre = pre_act[..., :hidden_units]
    up_pre = pre_act[..., hidden_units:]
    gated, derivative = silu_parts(gate_pre)
    hidden = (gated * up_pre).astype(jnp.bfloat16)
    expert_out = jnp.einsum(
        "sjcf,jfd->sjcd", hidden, down_weight, preferred_element_type=jnp.float32
    )
    slot_route = jnp.sum(grad_recv.astype(jnp.float32) * expert_out, axis=-1).astype(jnp.bfloat16)
    hid_grad = jnp.einsum("sjcd,jfd->sjcf", scaled, down_weight, preferred_element_type=jnp.float32)
    pre_grad = jnp.concatenate([hid_grad * up_pre * derivative, hid_grad * gated], axis=-1).astype(
        jnp.bfloat16
    )
    slot_grad = jnp.einsum(
        "sjcf,jdf->sjcd", pre_grad, up_weight, preferred_element_type=jnp.float32
    ).astype(jnp.bfloat16)
    up_grad = jnp.einsum(
        "sjcd,sjcf->jdf", tok_recv, pre_grad, preferred_element_type=jnp.float32
    ).astype(jnp.bfloat16)
    down_grad = jnp.einsum(
        "sjcf,sjcd->jfd", hidden, scaled, preferred_element_type=jnp.float32
    ).astype(jnp.bfloat16)
    grad_back, route_back = (
        lax.all_to_all(slot_grad, ("dp", "expert"), split_axis=0, concat_axis=0, tiled=True),
        lax.all_to_all(slot_route, ("dp", "expert"), split_axis=0, concat_axis=0, tiled=True),
    )
    grad_back = grad_back.reshape(slot_count, model_width)
    route_back = route_back.reshape(slot_count)
    token_grad = jnp.einsum(
        "ts,sd->td", dispatch, grad_back, preferred_element_type=jnp.float32
    ).astype(jnp.bfloat16)
    route_grad = (
        jnp.dot(placed, route_back, preferred_element_type=jnp.float32)
        .reshape(tok_rows, top_k)
        .astype(jnp.bfloat16)
    )
    return (token_grad, route_grad, up_grad, down_grad)


def solution(mesh):
    in_specs = (
        P(("dp", "expert"), None),
        P(("dp", "expert"), None),
        P(("dp", "expert"), None),
        P(("dp", "expert"), None),
        P(("dp", "expert"), None, None),
        P(("dp", "expert"), None, None),
    )
    out_specs = (
        P(("dp", "expert"), None),
        P(("dp", "expert"), None),
        P(("dp", "expert"), None, None),
        P(("dp", "expert"), None, None),
    )
    return jax.shard_map(local, mesh=mesh, in_specs=in_specs, out_specs=out_specs, check_vma=False)
```

profile of v0, /device:TPU:1, one launch (start us, length us, event | category | flops | bytes accessed | tf_op | source)
XLA Modules:
  0.0 257.6 jit_solution(6608054399061779564)
XLA Ops:
  0.6 0.9 copy.67
  1.8 0.8 copy.72
  3.9 0.8 reshape.170
  4.7 11.5 %all-to-all-start = ((bf16[128,1,6]{2,1,0:T(2,128)(2,1)}), bf16[128,1,6]{2,1,0:T(2,128)(2,1)S(1)}, u32[]{:S(2)}, u32[]{:S(2)}) async-start(bf16[128,1,6]{2,1,0:T(2,128)(2,1)} %reshape.170), calls=%async_computation | async-start | bytes 131072 | tf_op jit(solution)/shard_map/all_to_all | solution.py:57
  17.3 3.7 %convolution_convert_fusion = bf16[768,2048]{1,0:T(8,128)(2,1)} fusion(bf16[128,768]{1,0:T(8,128)(2,1)S(1)} %fusion.41, bf16[128,2048]{1,0:T(8,128)(2,1)} %param.6), kind=kOutput, calls=%fused_computation.12 | convolution fusion | flops 404226048 | bytes 3866624 | tf_op jit(solution)/shard_map/ts,td->sd/dot_general | solution.py:33
  21.0 6.2 %reshape.154 = bf16[128,1,6,2048]{3,2,0,1:T(8,128)(2,1)} reshape(bf16[768,2048]{1,0:T(8,128)(2,1)} %convolution_convert_fusion) | data formatting | bytes 6291456 | tf_op jit(solution)/shard_map/reshape | solution.py:44
  27.3 10.2 %all-to-all-start.2 = ((bf16[128,1,6,2048]{3,2,1,0:T(8,128)(2,1)}), bf16[128,1,6,2048]{3,2,1,0:T(8,128)(2,1)}, u32[]{:S(2)}, u32[]{:S(2)}) async-start(bf16[128,1,6,2048]{3,2,1,0:T(8,128)(2,1)} %bitcast.114), calls=%async_computation.2 | async-start | bytes 8388608 | tf_op jit(solution)/shard_map/all_to_all | solution.py:43
  37.5 3.7 %convolution_convert_fusion.1 = bf16[768,2048]{1,0:T(8,128)(2,1)} fusion(bf16[128,768]{1,0:T(8,128)(2,1)S(1)} %fusion.41, bf16[128,2048]{1,0:T(8,128)(2,1)} %param.7), kind=kOutput, calls=%fused_computation.13 | convolution fusion | flops 404226048 | bytes 3866624 | tf_op jit(solution)/shard_map/ts,td->sd/dot_general | solution.py:36
  41.2 6.3 %reshape.151 = bf16[128,1,6,2048]{3,2,0,1:T(8,128)(2,1)} reshape(bf16[768,2048]{1,0:T(8,128)(2,1)} %convolution_convert_fusion.1) | data formatting | bytes 6291456 | tf_op jit(solution)/shard_map/reshape | solution.py:51
  47.5 42.6 %all-to-all-done.2 = bf16[128,1,6,2048]{3,2,1,0:T(8,128)(2,1)} async-done(((bf16[128,1,6,2048]{3,2,1,0:T(8,128)(2,1)}), bf16[128,1,6,2048]{3,2,1,0:T(8,128)(2,1)}, u32[]{:S(2)}, u32[]{:S(2)}) %all-to-all-start.2) | async-done | bytes 3145760 | tf_op jit(solution)/shard_map/all_to_all | solution.py:43
  90.1 5.6 %all-to-all-start.1 = ((bf16[128,1,6,2048]{3,2,1,0:T(8,128)(2,1)}), bf16[128,1,6,2048]{3,2,1,0:T(8,128)(2,1)}, u32[]{:S(2)}, u32[]{:S(2)}) async-start(bf16[128,1,6,2048]{3,2,1,0:T(8,128)(2,1)} %bitcast.113), calls=%async_computation.1 | async-start | bytes 8388608 | tf_op jit(solution)/shard_map/all_to_all | solution.py:50
  95.9 15.7 %fusion.7 = f32[128,1,6,1536]{3,0,2,1:T(8,128)} fusion(bf16[1,2048,1536]{2,1,0:T(8,128)(2,1)} %param.10, bf16[128,1,6,2048]{3,2,1,0:T(8,128)(2,1)} %all-to-all-done.2), kind=kOutput, calls=%fused_computation.11 | convolution fusion | flops 4831838208 | bytes 14155776 | tf_op jit(solution)/shard_map/sjcd,jdf->sjcf/dot_general | solution.py:68
  111.5 36.9 %all-to-all-done.1 = bf16[128,1,6,2048]{3,2,1,0:T(8,128)(2,1)} async-done(((bf16[128,1,6,2048]{3,2,1,0:T(8,128)(2,1)}), bf16[128,1,6,2048]{3,2,1,0:T(8,128)(2,1)}, u32[]{:S(2)}, u32[]{:S(2)}) %all-to-all-start.1) | async-done | bytes 3145760 | tf_op jit(solution)/shard_map/all_to_all | solution.py:50
  148.5 11.3 %fusion.39 = (bf16[128,6,768]{2,0,1:T(8,128)(2,1)}, bf16[128,6,768]{2,0,1:T(8,128)(2,1)}, bf16[128,6,768]{2,0,1:T(8,128)(2,1)S(1)}) fusion(f32[128,1,6,1536]{3,0,2,1:T(8,128)} %fusion.7, bf16[1,768,2048]{2,1,0:T(8,128)(2,1)S(1)} %copy-done, f32[128,6]{0,1:T(8,128)S(1)} %copy.74, bf16[128,1,6,2048]{3,2,1,0:T(8,128)(2,1)} %all-to-all-done.1), kind=kOutput, calls=%fused_computation.45 | convolution fusion | flops 2429485056 | bytes 14552064 | tf_op jit(solution)/shard_map/sjcd,jfd->sjcf/dot_general | solution.py:77
  159.8 8.3 %fusion.2 = bf16[128,6]{0,1:T(8,128)(2,1)S(1)} fusion(bf16[128,6,768]{2,0,1:T(8,128)(2,1)S(1)} %get-tuple-element.6, bf16[1,768,2048]{2,1,0:T(8,128)(2,1)S(1)} %copy-done, bf16[128,1,6,2048]{3,2,1,0:T(8,128)(2,1)} %all-to-all-done.1), kind=kOutput, calls=%fused_computation.5 | convolution fusion | flops 2420636928 | bytes 7472640 | tf_op jit(solution)/shard_map/sjcf,jfd->sjcd/dot_general | solution.py:73
  168.9 4.5 %all-to-all-start.4 = ((bf16[128,1,6]{2,1,0:T(2,128)(2,1)}), bf16[128,1,6]{2,1,0:T(2,128)(2,1)S(1)}, u32[]{:S(2)}, u32[]{:S(2)}) async-start(bf16[128,1,6]{2,1,0:T(2,128)(2,1)} %copy.80), calls=%async_computation.4 | async-start | bytes 131072 | tf_op jit(solution)/shard_map/all_to_all | solution.py:92
  173.4 7.9 %fusion.20 = bf16[128,1,6,2048]{3,0,2,1:T(8,128)(2,1)S(1)} fusion(bf16[1,2048,1536]{2,1,0:T(8,128)(2,1)} %param.10, bf16[128,6,768]{2,0,1:T(8,128)(2,1)} %get-tuple-element.5, bf16[128,6,768]{2,0,1:T(8,128)(2,1)} %get-tuple-element.4), kind=kOutput, calls=%fused_computation.22 | convolution fusion | flops 4838129664 | bytes 11796480 | tf_op jit(solution)/shard_map/sjcf,jdf->sjcd/dot_general | solution.py:81
  181.3 3.7 %copy.79 = bf16[128,1,6,2048]{3,2,1,0:T(8,128)(2,1)} copy(bf16[128,1,6,2048]{3,0,2,1:T(8,128)(2,1)S(1)} %fusion.20) | data formatting | bytes 6291456 | tf_op jit(solution)/shard_map/convert_element_type | solution.py:83
  185.0 10.3 %all-to-all-start.3 = ((bf16[128,1,6,2048]{3,2,1,0:T(8,128)(2,1)}), bf16[128,1,6,2048]{3,2,1,0:T(8,128)(2,1)}, u32[]{:S(2)}, u32[]{:S(2)}) async-start(bf16[128,1,6,2048]{3,2,1,0:T(8,128)(2,1)} %copy.79), calls=%async_computation.3 | async-start | bytes 8388608 | tf_op jit(solution)/shard_map/all_to_all | solution.py:91
  195.3 11.8 %fusion.23 = bf16[1,768,2048]{2,1,0:T(8,128)(2,1)} fusion(bf16[128,6,768]{2,0,1:T(8,128)(2,1)S(1)} %copy-done.3, f32[128,6]{0,1:T(8,128)S(1)} %copy.74, bf16[128,1,6,2048]{3,2,1,0:T(8,128)(2,1)} %all-to-all-done.1), kind=kOutput, calls=%fused_computation.23 | convolution fusion | flops 2422210560 | bytes 7474176 | tf_op jit(solution)/shard_map/sjcf,sjcd->jfd/dot_general | solution.py:87
  207.2 14.2 %fusion = bf16[1,2048,1536]{2,1,0:T(8,128)(2,1)} fusion(bf16[128,6,2048]{2,1,0:T(8,128)(2,1)} %bitcast.34, bf16[128,6,768]{2,0,1:T(8,128)(2,1)S(1)} %copy-done.5, bf16[128,6,768]{2,0,1:T(8,128)(2,1)S(1)} %copy-done.4), kind=kOutput, calls=%fused_computation.3 | convolution fusion | flops 4839702528 | bytes 11796480 | tf_op jit(solution)/shard_map/sjcd,sjcf->jdf/dot_general | solution.py:84
  222.7 25.2 %all-to-all-done.3 = bf16[128,1,6,2048]{3,2,1,0:T(8,128)(2,1)} async-done(((bf16[128,1,6,2048]{3,2,1,0:T(8,128)(2,1)}), bf16[128,1,6,2048]{3,2,1,0:T(8,128)(2,1)}, u32[]{:S(2)}, u32[]{:S(2)}) %all-to-all-start.3) | async-done | bytes 3145760 | tf_op jit(solution)/shard_map/all_to_all | solution.py:91
  247.9 6.5 %reshape.157 = bf16[768,2048]{1,0:T(8,128)(2,1)} reshape(bf16[128,1,6,2048]{3,2,1,0:T(8,128)(2,1)} %all-to-all-done.3) | data formatting | bytes 6291456 | tf_op jit(solution)/shard_map/reshape | solution.py:94
  254.4 3.3 %convolution_convert_fusion.2 = bf16[128,2048]{1,0:T(8,128)(2,1)} fusion(bf16[128,768]{1,0:T(8,128)(2,1)S(1)} %fusion.41, bf16[768,2048]{1,0:T(8,128)(2,1)} %reshape.157), kind=kOutput, calls=%fused_computation.24 | convolution fusion | flops 402915328 | bytes 3866624 | tf_op jit(solution)/shard_map/ts,sd->td/dot_general | solution.py:96
  (38 shorter events, 4.8 us)
Async XLA Ops:
  0.6 147.8 %copy-start = (bf16[1,768,2048]{2,1,0:T(8,128)(2,1)S(1)}, bf16[1,768,2048]{2,1,0:T(8,128)(2,1)}, u32[]{:S(2)}) copy-start(bf16[1,768,2048]{2,1,0:T(8,128)(2,1)} %param.11) | copy-start | bytes 9437188
  4.7 22.6 %all-to-all-start = ((bf16[128,1,6]{2,1,0:T(2,128)(2,1)}), bf16[128,1,6]{2,1,0:T(2,128)(2,1)S(1)}, u32[]{:S(2)}, u32[]{:S(2)}) async-start(bf16[128,1,6]{2,1,0:T(2,128)(2,1)} %reshape.170), calls=%async_computation | async-start | bytes 131072 | tf_op jit(solution)/shard_map/all_to_all | solution.py:57
  27.3 62.8 %all-to-all-start.2 = ((bf16[128,1,6,2048]{3,2,1,0:T(8,128)(2,1)}), bf16[128,1,6,2048]{3,2,1,0:T(8,128)(2,1)}, u32[]{:S(2)}, u32[]{:S(2)}) async-start(bf16[128,1,6,2048]{3,2,1,0:T(8,128)(2,1)} %bitcast.114), calls=%async_computation.2 | async-start | bytes 8388608 | tf_op jit(solution)/shard_map/all_to_all | solution.py:43
  90.1 58.3 %all-to-all-start.1 = ((bf16[128,1,6,2048]{3,2,1,0:T(8,128)(2,1)}), bf16[128,1,6,2048]{3,2,1,0:T(8,128)(2,1)}, u32[]{:S(2)}, u32[]{:S(2)}) async-start(bf16[128,1,6,2048]{3,2,1,0:T(8,128)(2,1)} %bitcast.113), calls=%async_computation.1 | async-start | bytes 8388608 | tf_op jit(solution)/shard_map/all_to_all | solution.py:50
  159.8 8.3 %copy-start.2 = (bf16[128,6,768]{2,0,1:T(8,128)(2,1)}, bf16[128,6,768]{2,0,1:T(8,128)(2,1)S(1)}, u32[]{:S(2)}) copy-start(bf16[128,6,768]{2,0,1:T(8,128)(2,1)S(1)} %get-tuple-element.6) | copy-start | bytes 3538948
  168.9 16.1 %all-to-all-start.4 = ((bf16[128,1,6]{2,1,0:T(2,128)(2,1)}), bf16[128,1,6]{2,1,0:T(2,128)(2,1)S(1)}, u32[]{:S(2)}, u32[]{:S(2)}) async-start(bf16[128,1,6]{2,1,0:T(2,128)(2,1)} %copy.80), calls=%async_computation.4 | async-start | bytes 131072 | tf_op jit(solution)/shard_map/all_to_all | solution.py:92
  185.0 10.3 %copy-start.3 = (bf16[128,6,768]{2,0,1:T(8,128)(2,1)S(1)}, bf16[128,6,768]{2,0,1:T(8,128)(2,1)}, u32[]{:S(2)}) copy-start(bf16[128,6,768]{2,0,1:T(8,128)(2,1)} %copy-done.2) | copy-start | bytes 3538948
  185.0 62.9 %all-to-all-start.3 = ((bf16[128,1,6,2048]{3,2,1,0:T(8,128)(2,1)}), bf16[128,1,6,2048]{3,2,1,0:T(8,128)(2,1)}, u32[]{:S(2)}, u32[]{:S(2)}) async-start(bf16[128,1,6,2048]{3,2,1,0:T(8,128)(2,1)} %copy.79), calls=%async_computation.3 | async-start | bytes 8388608 | tf_op jit(solution)/shard_map/all_to_all | solution.py:91
  195.3 11.9 %copy-start.4 = (bf16[128,6,768]{2,0,1:T(8,128)(2,1)S(1)}, bf16[128,6,768]{2,0,1:T(8,128)(2,1)}, u32[]{:S(2)}) copy-start(bf16[128,6,768]{2,0,1:T(8,128)(2,1)} %get-tuple-element.4) | copy-start | bytes 3538948
  195.3 11.9 %copy-start.5 = (bf16[128,6,768]{2,0,1:T(8,128)(2,1)S(1)}, bf16[128,6,768]{2,0,1:T(8,128)(2,1)}, u32[]{:S(2)}) copy-start(bf16[128,6,768]{2,0,1:T(8,128)(2,1)} %get-tuple-element.5) | copy-start | bytes 3538948
  247.9 9.8 %copy-start.1 = (bf16[1,768,2048]{2,1,0:T(8,128)(2,1)S(1)}, bf16[1,768,2048]{2,1,0:T(8,128)(2,1)}, u32[]{:S(2)}) copy-start(bf16[1,768,2048]{2,1,0:T(8,128)(2,1)} %param.11) | copy-start | bytes 9437188
where the time goes:
time: 259 us; the launch traced here: 258 us
  waiting for transfers between devices  105 us (41%)
  matrix products  80.8 us (31%)
  starting transfers between devices  42.1 us (16%)
  local copies, waits for them, and re-layouts  26.9 us (10%)
    all_to_all x1, waiting for transfers between devices, local(): lax.all_to_all(tok_send.reshape(devices, local_experts, capacity, model_w...  42.6 us
    all_to_all x1, waiting for transfers between devices, local(): lax.all_to_all(grad_send.reshape(devices, local_experts, capacity, model_...  36.9 us
    all_to_all x1, waiting for transfers between devices, local(): lax.all_to_all(slot_grad, ('dp', 'expert'), split_axis=0, concat_axis=0,...  25.2 us
    dot_general x1, matrix products, local(): jnp.einsum('sjcd,jdf->sjcf', tok_recv, up_weight, preferred_element_type=...  15.7 us
    dot_general x1, matrix products, local(): jnp.einsum('sjcd,sjcf->jdf', tok_recv, pre_grad, preferred_element_type=j...  14.2 us
    dot_general x1, matrix products, local(): jnp.einsum('sjcf,sjcd->jfd', hidden, scaled, preferred_element_type=jnp.f...  11.8 us
    all_to_all x1, starting transfers between devices, local(): lax.all_to_all(weight_send.reshape(devices, local_experts, capacity), ('d...  11.5 us
    dot_general x1, matrix products, local(): jnp.einsum('sjcd,jfd->sjcf', scaled, down_weight, preferred_element_type=...  11.3 us
  transfers between devices with their start and end apart: 5, of which 3 were waited for; matrix products, arithmetic and copies ran while one was open for 29% of the time, Pallas kernels for 0%

commit v1 on v0

v1 whole, which is shorter than its diff:
```python
import jax
import jax.numpy as jnp
from jax import lax
from jax.experimental import pallas as pl
from jax.experimental.pallas import tpu as pltpu
from jax.sharding import PartitionSpec as P

AXES = ("dp", "expert")
TOK = 128
CAP = 6
D = 2048
FF = 768
MAIN = 1536
PIECE = 512
GROUP = 32
F32 = jnp.float32
BF16 = jnp.bfloat16


def dot(a, b):
    return jnp.dot(a, b, preferred_element_type=F32)


def dot_nt(a, b):
    return lax.dot_general(a, b, (((1,), (1,)), ((), ())), preferred_element_type=F32)


def dot_tn(a, b):
    return lax.dot_general(a, b, (((0,), (0,)), ((), ())), preferred_element_type=F32)


def chosen(ids, w):
    expert = lax.broadcasted_iota(jnp.int32, (TOK, TOK), 0)
    token = lax.broadcasted_iota(jnp.int32, (TOK, TOK), 1)
    hot = jnp.zeros((TOK, TOK), F32)
    weight = jnp.zeros((TOK, TOK), F32)
    for k in range(ids.shape[0]):
        named = expert == ids[k : k + 1, :]
        hot = hot + jnp.where(named, 1.0, 0.0)
        weight = weight + jnp.where(named, w[k : k + 1, :], 0.0)
    earlier = jnp.where(expert < token, 1.0, 0.0)
    before = dot(hot.astype(BF16), earlier.astype(BF16))
    return jnp.where(hot > 0.0, before, -9.0), weight


def spread(a):
    return jnp.broadcast_to(a[:, None, :], (a.shape[0], 8, TOK)).reshape(a.shape[0] * 8, TOK)


def slot_of_row(rows, piece):
    r = lax.broadcasted_iota(jnp.int32, (rows, TOK), 0) & 7
    if piece is None:
        return jnp.where(r < CAP, r, -5).astype(F32)
    return jnp.where(r >= CAP, 3 * (r - CAP) + piece, -5).astype(F32)


def dispatch_kernel(ids_ref, w_ref, tok_ref, grad_ref, out_ref, pos_ref, weight_ref, rows_ref):
    step = pl.program_id(0)

    @pl.when(step == 0)
    def _():
        pos, weight = chosen(ids_ref[...], w_ref[...].astype(F32))
        pos_ref[...] = pos
        weight_ref[...] = weight
        for a, ref in enumerate((tok_ref, grad_ref)):
            for j in range(3):
                rows_ref[a, j, :TOK, :] = ref[:, PIECE * j : PIECE * (j + 1)]
                rows_ref[a, j, TOK:, :] = ref[:, MAIN:]

    here = pl.ds(pl.multiple_of(step * GROUP, GROUP), GROUP)
    pos = spread(pos_ref[here, :])
    weight = spread(weight_ref[here, :])
    main = pos == slot_of_row(GROUP * 8, None)
    for j in range(3):
        part = pos == slot_of_row(GROUP * 8, j)
        for a in range(2):
            value = 1.0 if a == 0 else weight
            pick = jnp.concatenate(
                [jnp.where(main, value, 0.0).astype(BF16), jnp.where(part, value, 0.0).astype(BF16)], axis=1
            )
            at = MAIN * a + PIECE * j
            out_ref[:, at : at + PIECE] = dot(pick, rows_ref[a, j]).astype(BF16)


def dispatch(ids, w, tokens, grads):
    whole = lambda shape: pl.BlockSpec(shape, lambda i: (0, 0))
    return pl.pallas_call(
        dispatch_kernel,
        grid=(TOK // GROUP,),
        out_shape=jax.ShapeDtypeStruct((TOK * 8, 2 * MAIN), BF16),
        in_specs=[whole(ids.shape), whole(w.shape), whole(tokens.shape), whole(grads.shape)],
        out_specs=pl.BlockSpec((GROUP * 8, 2 * MAIN), lambda i: (i, 0)),
        scratch_shapes=[
            pltpu.VMEM((TOK, TOK), F32),
            pltpu.VMEM((TOK, TOK), F32),
            pltpu.VMEM((2, 3, 2 * TOK, PIECE), BF16),
        ],
        compiler_params=pltpu.CompilerParams(vmem_limit_bytes=24 * 2**20),
        cost_estimate=pl.CostEstimate(flops=1610612736, bytes_accessed=7340032, transcendentals=0),
        name="dispatch",
    )(ids, w, tokens, grads)


def pack_match(rows, columns, row_axis, piece):
    m = lax.broadcasted_iota(jnp.int32, (rows, columns), row_axis)
    s = lax.broadcasted_iota(jnp.int32, (rows, columns), 1 - row_axis)
    r = m & 7
    first = CAP * (m >> 3)
    if piece is None:
        hit = (s == first + r) & (r < CAP)
    else:
        hit = (s == first + 3 * (r - CAP) + piece) & (r >= CAP)
    return jnp.where(hit, 1.0, 0.0).astype(BF16)


def middle_kernel(
    recv_hbm, up_hbm, down_hbm, x_hbm, s_hbm, hidden_hbm, pre_grad_hbm, back_hbm, route_ref,
    recv, up, down, x, s, hidden, pre_grad, tail, back, in_sem, w_sem, out_sem,
):
    rows, slots = 8 * GROUP, CAP * GROUP
    total = CAP * TOK
    groups = TOK // GROUP
    arrive = [
        pltpu.make_async_copy(recv_hbm.at[pl.ds(rows * g, rows), :], recv.at[pl.ds(rows * g, rows), :], in_sem.at[g])
        for g in range(groups)
    ]
    up_copy = pltpu.make_async_copy(up_hbm, up, w_sem.at[0])
    down_copy = pltpu.make_async_copy(down_hbm, down, w_sem.at[1])
    for c in arrive:
        c.start()
    up_copy.start()
    down_copy.start()
    take = [pack_match(slots, rows, 1, piece) for piece in (None, 0, 1, 2)]
    for g in range(groups):
        arrive[g].wait()
        here = pl.ds(slots * g, slots)
        there = pl.ds(rows * g, rows)
        for a, ref in enumerate((x, s)):
            ref[here, :MAIN] = dot(take[0], recv[there, MAIN * a : MAIN * (a + 1)]).astype(BF16)
            last = jnp.zeros((slots, PIECE), F32)
            for j in range(3):
                at = MAIN * a + PIECE * j
                last = last + dot(take[1 + j], recv[there, at : at + PIECE])
            ref[here, MAIN:] = last.astype(BF16)
    out_x = pltpu.make_async_copy(x, x_hbm, out_sem.at[0])
    out_s = pltpu.make_async_copy(s, s_hbm, out_sem.at[1])
    out_x.start()
    out_s.start()
    up_copy.wait()
    down_copy.wait()
    route = jnp.zeros((total, 1), F32)
    width = 256
    for n in range(FF // width):
        at = width * n
        gate = dot(x[...], up[:, at : at + width])
        lift = dot(x[...], up[:, FF + at : FF + at + width])
        hid_grad = dot_nt(s[...], down[at : at + width, :])
        sigma = jax.nn.sigmoid(gate)
        gated = gate * sigma
        derivative = sigma * (1.0 + gate * (1.0 - sigma))
        hid = (gated * lift).astype(BF16)
        hidden[:, at : at + width] = hid
        route = route + jnp.sum(hid.astype(F32) * hid_grad, axis=1, keepdims=True)
        pre_grad[:, at : at + width] = (hid_grad * lift * derivative).astype(BF16)
        pre_grad[:, FF + at : FF + at + width] = (hid_grad * gated).astype(BF16)
    out_h = pltpu.make_async_copy(hidden, hidden_hbm, out_sem.at[2])
    out_p = pltpu.make_async_copy(pre_grad, pre_grad_hbm, out_sem.at[3])
    out_h.start()
    out_p.start()
    slot = lax.broadcasted_iota(jnp.int32, (total, TOK), 0)
    block = lax.broadcasted_iota(jnp.int32, (total, TOK), 1)
    offset = slot - CAP * block
    for c in range(8):
        route_ref[c : c + 1, :] = jnp.sum(jnp.where((offset == c) & (c < CAP), route, 0.0), axis=0, keepdims=True)
    put = [pack_match(rows, slots, 0, piece) for piece in (None, 0, 1, 2)]
    tail[...] = dot_nt(pre_grad[...], up[MAIN:, :]).astype(BF16)
    leave = []
    for j in range(3):
        at = PIECE * j
        grad = dot_nt(pre_grad[...], up[at : at + PIECE, :]).astype(BF16)
        for g in range(groups):
            packed = dot(put[0], grad[slots * g : slots * (g + 1), :])
            packed = packed + dot(put[1 + j], tail[slots * g : slots * (g + 1), :])
            back[rows * g : rows * (g + 1), at : at + PIECE] = packed.astype(BF16)
        c = pltpu.make_async_copy(
            back.at[:, pl.ds(at, PIECE)], back_hbm.at[:, pl.ds(at, PIECE)], out_sem.at[4 + j]
        )
        c.start()
        leave.append(c)
    for c in [out_x, out_s, out_h, out_p] + leave:
        c.wait()


def middle(recv, up, down):
    total = CAP * TOK
    hbm = pl.BlockSpec(memory_space=pl.ANY)
    shapes = [
        jax.ShapeDtypeStruct((total, D), BF16),
        jax.ShapeDtypeStruct((total, D), BF16),
        jax.ShapeDtypeStruct((total, FF), BF16),
        jax.ShapeDtypeStruct((total, 2 * FF), BF16),
        jax.ShapeDtypeStruct((TOK * 8, MAIN), BF16),
        jax.ShapeDtypeStruct((8, TOK), F32),
    ]
    return pl.pallas_call(
        middle_kernel,
        out_shape=shapes,
        in_specs=[hbm] * 3,
        out_specs=[hbm] * 5 + [pl.BlockSpec(memory_space=pltpu.VMEM)],
        scratch_shapes=[
            pltpu.VMEM((TOK * 8, 2 * MAIN), BF16),
            pltpu.VMEM((D, 2 * FF), BF16),
            pltpu.VMEM((FF, D), BF16),
            pltpu.VMEM((total, D), BF16),
            pltpu.VMEM((total, D), BF16),
            pltpu.VMEM((total, FF), BF16),
            pltpu.VMEM((total, 2 * FF), BF16),
            pltpu.VMEM((total, PIECE), BF16),
            pltpu.VMEM((TOK * 8, MAIN), BF16),
            pltpu.SemaphoreType.DMA((TOK // GROUP,)),
            pltpu.SemaphoreType.DMA((2,)),
            pltpu.SemaphoreType.DMA((7,)),
        ],
        compiler_params=pltpu.CompilerParams(vmem_limit_bytes=56 * 2**20),
        cost_estimate=pl.CostEstimate(flops=16 * 10**9, bytes_accessed=29 * 10**6, transcendentals=589824),
        name="middle",
    )(recv, up, down)


def combine_kernel(me_ref, ids_ref, w_ref, back_ref, sums_ref, token_ref, route_ref):
    ids = ids_ref[...]
    w = w_ref[...].astype(F32)
    pos, _ = chosen(ids, w)
    pos = spread(pos)
    main = pos == slot_of_row(TOK * 8, None)
    last = jnp.zeros((TOK, PIECE), F32)
    for j in range(3):
        part = pos == slot_of_row(TOK * 8, j)
        pick = jnp.concatenate(
            [jnp.where(main, 1.0, 0.0).astype(BF16), jnp.where(part, 1.0, 0.0).astype(BF16)], axis=1
        )
        both = dot_tn(pick, back_ref[:, PIECE * j : PIECE * (j + 1)])
        token_ref[:, PIECE * j : PIECE * (j + 1)] = both[:TOK].astype(BF16)
        last = last + both[TOK:]
    token_ref[:, MAIN:] = last.astype(BF16)
    lane = lax.broadcasted_iota(jnp.int32, (TOK * 8, TOK), 1)
    mine = jnp.sum(jnp.where(lane == me_ref[0], sums_ref[...], 0.0), axis=1, keepdims=True)
    held = jnp.where(main, mine, 0.0)
    expert = lax.broadcasted_iota(jnp.int32, (TOK * 8, TOK), 0) >> 3
    for k in range(ids.shape[0]):
        found = jnp.sum(jnp.where(expert == ids[k : k + 1, :], held, 0.0), axis=0, keepdims=True)
        route_ref[k : k + 1, :] = (found / w[k : k + 1, :]).astype(BF16)


def combine(me, ids, w, back, sums):
    vmem = pl.BlockSpec(memory_space=pltpu.VMEM)
    return pl.pallas_call(
        combine_kernel,
        out_shape=[jax.ShapeDtypeStruct((TOK, D), BF16), jax.ShapeDtypeStruct(ids.shape, BF16)],
        in_specs=[pl.BlockSpec(memory_space=pltpu.SMEM)] + [vmem] * 4,
        out_specs=[vmem] * 2,
        compiler_params=pltpu.CompilerParams(vmem_limit_bytes=24 * 2**20),
        cost_estimate=pl.CostEstimate(flops=805306368, bytes_accessed=4 * 10**6, transcendentals=0),
        name="combine",
    )(me, ids, w, back, sums)


def exchange(a):
    return lax.all_to_all(a, AXES, split_axis=0, concat_axis=0, tiled=True)


def local(tokens, out_grad, expert_ids, route_weight, up_weight, down_weight):
    ids = expert_ids.T
    w = route_weight.T
    send = dispatch(ids, w, tokens, out_grad)
    recv = exchange(send.reshape(TOK, 8, 2 * MAIN)).reshape(TOK * 8, 2 * MAIN)
    x, s, hidden, pre_grad, back, sums = middle(recv, up_weight[0], down_weight[0])
    back = exchange(back.reshape(TOK, 8, MAIN)).reshape(TOK * 8, MAIN)
    sums = lax.all_gather(sums, AXES, axis=0, tiled=True)
    up_grad = dot_tn(x, pre_grad).astype(BF16)[None]
    down_grad = dot_tn(hidden, s).astype(BF16)[None]
    me = (lax.axis_index("dp") * lax.axis_size("expert") + lax.axis_index("expert")).astype(jnp.int32)
    token_grad, route_grad = combine(me.reshape(1), ids, w, back, sums)
    return token_grad, route_grad.T, up_grad, down_grad


def solution(mesh):
    two = P(AXES, None)
    three = P(AXES, None, None)
    return jax.shard_map(
        local,
        mesh=mesh,
        in_specs=(two, two, two, two, three, three),
        out_specs=(two, two, three, three),
        check_vma=False,
    )
```

time: 259 us -> 208 us (0.80)
  blocking collectives: 0 us -> 155 us
  waiting for transfers between devices: 105 us -> 0.01 us
  matrix products: 80.8 us -> 13.8 us
  starting transfers between devices: 42.1 us -> 4.74 us
  Pallas kernels: 0 us -> 28.4 us
  local copies, waits for them, and re-layouts: 26.9 us -> 4.49 us
    all_to_all x5 -> x1, waiting for transfers between devices: 105 us -> 0.01 us  [exchange(): return lax.all_to_all(a, AXES, split_axis=0, concat_axis=0, tiled=True)]
    all_to_all x0 -> x1, blocking collectives: none -> 86.6 us  [exchange(): return lax.all_to_all(a, AXES, split_axis=0, concat_axis=0, tiled=True)]
    all_gather x0 -> x1, blocking collectives: none -> 68.6 us  [local(): sums = lax.all_gather(sums, AXES, axis=0, tiled=True)]
    dot_general x11 -> x2, matrix products: 80.8 us -> 13.8 us  [dot_tn(): lax.dot_general(a, b, (((0,), (0,)), ((), ())), preferred_element_type=F32)]
    all_to_all x5 -> x1, starting transfers between devices: 42.1 us -> 4.74 us  [exchange(): return lax.all_to_all(a, AXES, split_axis=0, concat_axis=0, tiled=True)]
    pallas_call x0 -> x3, Pallas kernels: none -> 28.4 us  [the longest x1 23.5 us: middle(): pl.pallas_call(middle_kernel, out_shape=shapes, in_specs=[hbm] * 3, out_s...]
    reshape x6 -> x0, local copies, waits for them, and re-layouts: 20.1 us -> none  [the longest x1 6.49 us: local(): grad_back = grad_back.reshape(slot_count, model_width)]
    convert_element_type x2 -> x0, local copies, waits for them, and re-layouts: 4.49 us -> none  [the longest x1 3.72 us: local(): slot_grad = jnp.einsum('sjcf,jdf->sjcd', pre_grad, up_weight, preferred_e...]
  transfers between devices with their start and end apart: 5 -> 1, of which waited for: 3 -> 0; matrix products, arithmetic and copies ran while one was open for 29% -> 7% of each run, Pallas kernels for 0% -> 0%
where the time goes in v1:
time: 208 us; the launch traced here: 207 us
  blocking collectives  155 us (75%)
  Pallas kernels  28.4 us (14%)
  matrix products  13.8 us (7%)
  starting transfers between devices  4.74 us (2%)
  local copies, waits for them, and re-layouts  4.49 us (2%)
    all_to_all x1, blocking collectives, exchange(): return lax.all_to_all(a, AXES, split_axis=0, concat_axis=0, tiled=True)  86.6 us
    all_gather x1, blocking collectives, local(): sums = lax.all_gather(sums, AXES, axis=0, tiled=True)  68.6 us
    pallas_call x1, Pallas kernels, middle(): pl.pallas_call(middle_kernel, out_shape=shapes, in_specs=[hbm] * 3, out_s...  23.5 us
    dot_general x2, matrix products, dot_tn(): lax.dot_general(a, b, (((0,), (0,)), ((), ())), preferred_element_type=F32)  13.8 us
    all_to_all x1, starting transfers between devices, exchange(): return lax.all_to_all(a, AXES, split_axis=0, concat_axis=0, tiled=True)  4.74 us
    unnamed x20, local copies, waits for them, and re-layouts  4.49 us
  transfers between devices with their start and end apart: 1, of which 0 were waited for; matrix products, arithmetic and copies ran while one was open for 7% of the time, Pallas kernels for 0%

profile of v1, /device:TPU:1, one launch (start us, length us, event | category | flops | bytes accessed | tf_op | source)
XLA Modules:
  0.0 207.3 jit_solution(8747821927849549423)
XLA Ops:
  0.6 0.0 copy-start.1
  0.6 1.0 copy-done.1
  1.7 0.0 copy-start.2
  1.7 1.0 copy-done.2
  2.7 0.7 copy-done.3
  3.4 0.7 copy-done.5
  4.1 2.5 %dispatch.1 = bf16[1024,3072]{1,0:T(8,128)(2,1)S(1)} custom-call(s32[4,128]{1,0:T(4,128)S(1)} %bitcast.20, bf16[4,128]{1,0:T(4,128)(2,1)S(1)} %bitcast.22, bf16[128,2048]{1,0:T(8,128)(2,1)S(1)} %copy-done.1, bf16[128,2048]{1,0:T(8,128)(2,1)S(1)} %copy-done.2), custom_call_target="tpu_custom_call" | custom-call | flops 1610612736 | bytes 7340032 | tf_op jit(solution)/shard_map/dispatch/pallas_call | solution.py:87
  6.6 86.6 %all_to_all.10 = bf16[128,8,3072]{2,1,0:T(8,128)(2,1)} all-to-all(bf16[128,8,3072]{2,1,0:T(8,128)(2,1)S(1)} %bitcast.18), channel_id=1, replica_groups=mesh['dp'=4,'expert'=32] {'dp','expert'}, dimensions={0} | all-to-all | bytes 12582912 | tf_op jit(solution)/shard_map/all_to_all | solution.py:269
  93.2 23.5 %middle.1 = (bf16[768,2048]{1,0:T(8,128)(2,1)}, bf16[768,2048]{1,0:T(8,128)(2,1)}, bf16[768,768]{1,0:T(8,128)(2,1)}, bf16[768,1536]{1,0:T(8,128)(2,1)}, bf16[1024,1536]{1,0:T(8,128)(2,1)}, /*index=5*/f32[8,128]{1,0:T(8,128)}) custom-call(bf16[1024,3072]{1,0:T(8,128)(2,1)} %bitcast.24, bf16[2048,1536]{1,0:T(8,128)(2,1)} %bitcast.26, bf16[768,2048]{1,0:T(8,128)(2,1)} %bitcast.27), custom_call_target="tpu_custom_call" | custom-call | flops 16000000000 | bytes 29000000 | tf_op jit(solution)/shard_map/middle/pallas_call | solution.py:205
  116.8 0.0 copy-start.7
  116.8 4.7 %all-to-all-start.1 = ((bf16[128,8,1536]{2,1,0:T(8,128)(2,1)}), bf16[128,8,1536]{2,1,0:T(8,128)(2,1)S(1)}, u32[]{:S(2)}, u32[]{:S(2)}) async-start(bf16[128,8,1536]{2,1,0:T(8,128)(2,1)} %bitcast.25), calls=%async_computation.1 | async-start | bytes 6291456 | tf_op jit(solution)/shard_map/all_to_all | solution.py:269
  121.5 0.0 copy-done.7
  121.5 68.6 %all_gather.3.sums_ref = f32[1024,128]{1,0:T(8,128)} all-gather(f32[8,128]{1,0:T(8,128)S(1)} %copy-done.7), channel_id=1, replica_groups=mesh['dp'=4,'expert'=32] {'dp','expert'}, dimensions={0}, use_global_device_ids=true | all-gather | bytes 528384 | tf_op jit(solution)/shard_map/all_gather | solution.py:279
  190.1 6.7 %fusion.1 = bf16[1,768,2048]{2,1,0:T(8,128)(2,1)} fusion(bf16[768,768]{1,0:T(8,128)(2,1)} %get-tuple-element.18, bf16[768,2048]{1,0:T(8,128)(2,1)} %get-tuple-element.19), kind=kOutput, calls=%fused_computation.3 | convolution fusion | flops 2417491968 | bytes 7471104 | tf_op jit(solution)/shard_map/dot_general | solution.py:29
  196.8 0.0 copy-done.8
  196.9 0.0 copy-done.9
  196.9 0.0 copy-start.6
  196.9 7.1 %fusion = bf16[1,2048,1536]{2,1,0:T(8,128)(2,1)} fusion(bf16[768,2048]{1,0:T(8,128)(2,1)S(1)} %copy-done.8, bf16[768,1536]{1,0:T(8,128)(2,1)S(1)} %copy-done.9), kind=kOutput, calls=%fused_computation.1 | convolution fusion | flops 4834983936 | bytes 11796480 | tf_op jit(solution)/shard_map/dot_general | solution.py:29
  204.0 0.0 all-to-all-done.1
  204.0 0.0 copy-done.4
  204.0 0.0 copy-done.6
  204.0 0.0 copy-start
  204.0 1.0 copy-done
  205.0 2.3 %combine.1 = (bf16[128,2048]{1,0:T(8,128)(2,1)}, bf16[4,128]{1,0:T(4,128)(2,1)}) custom-call(s32[1]{0:T(128)} %bitcast.me_ref, s32[4,128]{1,0:T(4,128)S(1)} %bitcast.21, bf16[4,128]{1,0:T(4,128)(2,1)S(1)} %bitcast.23, bf16[1024,1536]{1,0:T(8,128)(2,1)S(1)} %bitcast.19, f32[1024,128]{1,0:T(8,128)S(1)} %copy-done), custom_call_target="tpu_custom_call" | custom-call | flops 805306368 | bytes 4000000 | tf_op jit(solution)/shard_map/combine/pallas_call | solution.py:257
  (5 shorter events, 0.0 us)
Async XLA Ops:
  0.6 1.0 copy-start.1
  1.7 1.0 copy-start.2
  2.7 0.7 copy-start.3
  3.4 0.7 copy-start.5
  116.8 4.8 %copy-start.7 = (f32[8,128]{1,0:T(8,128)S(1)}, f32[8,128]{1,0:T(8,128)}, u32[]{:S(2)}) copy-start(f32[8,128]{1,0:T(8,128)} %get-tuple-element.13) | copy-start | bytes 12292
  116.8 87.2 %all-to-all-start.1 = ((bf16[128,8,1536]{2,1,0:T(8,128)(2,1)}), bf16[128,8,1536]{2,1,0:T(8,128)(2,1)S(1)}, u32[]{:S(2)}, u32[]{:S(2)}) async-start(bf16[128,8,1536]{2,1,0:T(8,128)(2,1)} %bitcast.25), calls=%async_computation.1 | async-start | bytes 6291456 | tf_op jit(solution)/shard_map/all_to_all | solution.py:269
  190.1 6.7 %copy-start.8 = (bf16[768,2048]{1,0:T(8,128)(2,1)S(1)}, bf16[768,2048]{1,0:T(8,128)(2,1)}, u32[]{:S(2)}) copy-start(bf16[768,2048]{1,0:T(8,128)(2,1)} %get-tuple-element.16) | copy-start | bytes 9437188
  190.1 6.7 %copy-start.9 = (bf16[768,1536]{1,0:T(8,128)(2,1)S(1)}, bf16[768,1536]{1,0:T(8,128)(2,1)}, u32[]{:S(2)}) copy-start(bf16[768,1536]{1,0:T(8,128)(2,1)} %get-tuple-element.17) | copy-start | bytes 7077892
  196.9 7.1 %copy-start.4 = (s32[128,4]{0,1:T(4,128)S(1)}, s32[128,4]{0,1:T(4,128)}, u32[]{:S(2)}) copy-start(s32[128,4]{0,1:T(4,128)} %param.8) | copy-start | bytes 6148
  196.9 7.1 %copy-start.6 = (bf16[128,4]{0,1:T(4,128)(2,1)S(1)}, bf16[128,4]{0,1:T(4,128)(2,1)}, u32[]{:S(2)}) copy-start(bf16[128,4]{0,1:T(4,128)(2,1)} %param.9) | copy-start | bytes 3076
  204.0 1.0 copy-start

commit v2 on v1

--- a/solution.py
+++ b/solution.py
@@ -12,6 +12,7 @@
 FF = 768
 MAIN = 1536
 PIECE = 512
+SUMS = 128
 GROUP = 32
 F32 = jnp.float32
 BF16 = jnp.bfloat16
@@ -95,7 +96,7 @@
             pltpu.VMEM((TOK, TOK), F32),
             pltpu.VMEM((2, 3, 2 * TOK, PIECE), BF16),
         ],
-        compiler_params=pltpu.CompilerParams(vmem_limit_bytes=24 * 2**20),
+        compiler_params=pltpu.CompilerParams(vmem_limit_bytes=56 * 2**20),
         cost_estimate=pl.CostEstimate(flops=1610612736, bytes_accessed=7340032, transcendentals=0),
         name="dispatch",
     )(ids, w, tokens, grads)
@@ -114,7 +115,7 @@
 
 
 def middle_kernel(
-    recv_hbm, up_hbm, down_hbm, x_hbm, s_hbm, hidden_hbm, pre_grad_hbm, back_hbm, route_ref,
+    recv_hbm, up_hbm, down_hbm, x_hbm, s_hbm, hidden_hbm, pre_grad_hbm, back_hbm,
     recv, up, down, x, s, hidden, pre_grad, tail, back, in_sem, w_sem, out_sem,
 ):
     rows, slots = 8 * GROUP, CAP * GROUP
@@ -167,14 +168,15 @@
     out_p = pltpu.make_async_copy(pre_grad, pre_grad_hbm, out_sem.at[3])
     out_h.start()
     out_p.start()
-    slot = lax.broadcasted_iota(jnp.int32, (total, TOK), 0)
-    block = lax.broadcasted_iota(jnp.int32, (total, TOK), 1)
-    offset = slot - CAP * block
-    for c in range(8):
-        route_ref[c : c + 1, :] = jnp.sum(jnp.where((offset == c) & (c < CAP), route, 0.0), axis=0, keepdims=True)
     put = [pack_match(rows, slots, 0, piece) for piece in (None, 0, 1, 2)]
+    high = route.astype(BF16).astype(F32)
+    lane = lax.broadcasted_iota(jnp.int32, (total, SUMS), 1)
+    sums = jnp.where(lane == 0, high, jnp.where(lane == 1, route - high, 0.0)).astype(BF16)
+    for g in range(groups):
+        back[rows * g : rows * (g + 1), MAIN:] = dot(put[0], sums[slots * g : slots * (g + 1), :]).astype(BF16)
     tail[...] = dot_nt(pre_grad[...], up[MAIN:, :]).astype(BF16)
-    leave = []
+    leave = [pltpu.make_async_copy(back.at[:, pl.ds(MAIN, SUMS)], back_hbm.at[:, pl.ds(MAIN, SUMS)], out_sem.at[7])]
+    leave[0].start()
     for j in range(3):
         at = PIECE * j
         grad = dot_nt(pre_grad[...], up[at : at + PIECE, :]).astype(BF16)
@@ -199,14 +201,13 @@
         jax.ShapeDtypeStruct((total, D), BF16),
         jax.ShapeDtypeStruct((total, FF), BF16),
         jax.ShapeDtypeStruct((total, 2 * FF), BF16),
-        jax.ShapeDtypeStruct((TOK * 8, MAIN), BF16),
-        jax.ShapeDtypeStruct((8, TOK), F32),
+        jax.ShapeDtypeStruct((TOK * 8, MAIN + SUMS), BF16),
     ]
     return pl.pallas_call(
         middle_kernel,
         out_shape=shapes,
         in_specs=[hbm] * 3,
-        out_specs=[hbm] * 5 + [pl.BlockSpec(memory_space=pltpu.VMEM)],
+        out_specs=[hbm] * 5,
         scratch_shapes=[
             pltpu.VMEM((TOK * 8, 2 * MAIN), BF16),
             pltpu.VMEM((D, 2 * FF), BF16),
@@ -216,10 +217,10 @@
             pltpu.VMEM((total, FF), BF16),
             pltpu.VMEM((total, 2 * FF), BF16),
             pltpu.VMEM((total, PIECE), BF16),
-            pltpu.VMEM((TOK * 8, MAIN), BF16),
+            pltpu.VMEM((TOK * 8, MAIN + SUMS), BF16),
             pltpu.SemaphoreType.DMA((TOK // GROUP,)),
             pltpu.SemaphoreType.DMA((2,)),
-            pltpu.SemaphoreType.DMA((7,)),
+            pltpu.SemaphoreType.DMA((8,)),
         ],
         compiler_params=pltpu.CompilerParams(vmem_limit_bytes=56 * 2**20),
         cost_estimate=pl.CostEstimate(flops=16 * 10**9, bytes_accessed=29 * 10**6, transcendentals=589824),
@@ -227,7 +228,7 @@
     )(recv, up, down)
 
 
-def combine_kernel(me_ref, ids_ref, w_ref, back_ref, sums_ref, token_ref, route_ref):
+def combine_kernel(ids_ref, w_ref, back_ref, token_ref, route_ref):
     ids = ids_ref[...]
     w = w_ref[...].astype(F32)
     pos, _ = chosen(ids, w)
@@ -243,8 +244,7 @@
         token_ref[:, PIECE * j : PIECE * (j + 1)] = both[:TOK].astype(BF16)
         last = last + both[TOK:]
     token_ref[:, MAIN:] = last.astype(BF16)
-    lane = lax.broadcasted_iota(jnp.int32, (TOK * 8, TOK), 1)
-    mine = jnp.sum(jnp.where(lane == me_ref[0], sums_ref[...], 0.0), axis=1, keepdims=True)
+    mine = jnp.sum(back_ref[:, MAIN:].astype(F32), axis=1, keepdims=True)
     held = jnp.where(main, mine, 0.0)
     expert = lax.broadcasted_iota(jnp.int32, (TOK * 8, TOK), 0) >> 3
     for k in range(ids.shape[0]):
@@ -252,17 +252,17 @@
         route_ref[k : k + 1, :] = (found / w[k : k + 1, :]).astype(BF16)
 
 
-def combine(me, ids, w, back, sums):
+def combine(ids, w, back):
     vmem = pl.BlockSpec(memory_space=pltpu.VMEM)
     return pl.pallas_call(
         combine_kernel,
         out_shape=[jax.ShapeDtypeStruct((TOK, D), BF16), jax.ShapeDtypeStruct(ids.shape, BF16)],
-        in_specs=[pl.BlockSpec(memory_space=pltpu.SMEM)] + [vmem] * 4,
+        in_specs=[vmem] * 3,
         out_specs=[vmem] * 2,
         compiler_params=pltpu.CompilerParams(vmem_limit_bytes=24 * 2**20),
         cost_estimate=pl.CostEstimate(flops=805306368, bytes_accessed=4 * 10**6, transcendentals=0),
         name="combine",
-    )(me, ids, w, back, sums)
+    )(ids, w, back)
 
 
 def exchange(a):
@@ -274,13 +274,11 @@
     w = route_weight.T
     send = dispatch(ids, w, tokens, out_grad)
     recv = exchange(send.reshape(TOK, 8, 2 * MAIN)).reshape(TOK * 8, 2 * MAIN)
-    x, s, hidden, pre_grad, back, sums = middle(recv, up_weight[0], down_weight[0])
-    back = exchange(back.reshape(TOK, 8, MAIN)).reshape(TOK * 8, MAIN)
-    sums = lax.all_gather(sums, AXES, axis=0, tiled=True)
+    x, s, hidden, pre_grad, back = middle(recv, up_weight[0], down_weight[0])
+    back = exchange(back.reshape(TOK, 8, MAIN + SUMS)).reshape(TOK * 8, MAIN + SUMS)
     up_grad = dot_tn(x, pre_grad).astype(BF16)[None]
     down_grad = dot_tn(hidden, s).astype(BF16)[None]
-    me = (lax.axis_index("dp") * lax.axis_size("expert") + lax.axis_index("expert")).astype(jnp.int32)
-    token_grad, route_grad = combine(me.reshape(1), ids, w, back, sums)
+    token_grad, route_grad = combine(ids, w, back)
     return token_grad, route_grad.T, up_grad, down_grad
 
 

time: 208 us -> 168 us (0.81)
  blocking collectives: 155 us -> 86.8 us
  waiting for transfers between devices: 0.01 us -> 30.5 us
  local copies, waits for them, and re-layouts: 4.49 us -> 0.02 us
  Pallas kernels: 28.4 us -> 31.6 us
    all_gather x1 -> x0, blocking collectives: 68.6 us -> none  [local(): sums = lax.all_gather(sums, AXES, axis=0, tiled=True)]
    all_to_all x1, waiting for transfers between devices: 0.01 us -> 30.5 us  [exchange(): return lax.all_to_all(a, AXES, split_axis=0, concat_axis=0, tiled=True)]
    unnamed x20 -> x8, local copies, waits for them, and re-layouts: 4.49 us -> 0.02 us
    pallas_call x1, Pallas kernels: 2.54 us -> 5.49 us  [dispatch(): pl.pallas_call(dispatch_kernel, grid=(TOK // GROUP,), out_shape=jax.Shape...]
  transfers between devices with their start and end apart: 1 -> 1, of which waited for: 0 -> 1; matrix products, arithmetic and copies ran while one was open for 7% -> 8% of each run, Pallas kernels for 0% -> 0%
where the time goes in v2:
time: 168 us
  blocking collectives  86.8 us (52%)
  Pallas kernels  31.6 us (19%)
  waiting for transfers between devices  30.5 us (18%)
  matrix products  13.8 us (8%)
  starting transfers between devices  4.75 us (3%)
    all_to_all x1, blocking collectives, exchange(): return lax.all_to_all(a, AXES, split_axis=0, concat_axis=0, tiled=True)  86.8 us
    all_to_all x1, waiting for transfers between devices, exchange(): return lax.all_to_all(a, AXES, split_axis=0, concat_axis=0, tiled=True)  30.5 us
    pallas_call x1, Pallas kernels, middle(): pl.pallas_call(middle_kernel, out_shape=shapes, in_specs=[hbm] * 3, out_s...  23.8 us
    dot_general x2, matrix products, dot_tn(): lax.dot_general(a, b, (((0,), (0,)), ((), ())), preferred_element_type=F32)  13.8 us
    pallas_call x1, Pallas kernels, dispatch(): pl.pallas_call(dispatch_kernel, grid=(TOK // GROUP,), out_shape=jax.Shape...  5.49 us
    all_to_all x1, starting transfers between devices, exchange(): return lax.all_to_all(a, AXES, split_axis=0, concat_axis=0, tiled=True)  4.75 us
  transfers between devices with their start and end apart: 1, of which 1 were waited for; matrix products, arithmetic and copies ran while one was open for 8% of the time, Pallas kernels for 0%

profile of v2, /device:TPU:1, one launch (start us, length us, event | category | flops | bytes accessed | tf_op | source)
XLA Modules:
  0.0 168.2 jit_solution(13455652982285495392)
XLA Ops:
  0.6 5.5 %dispatch.1 = bf16[1024,3072]{1,0:T(8,128)(2,1)} custom-call(s32[4,128]{1,0:T(4,128)} %bitcast.18, bf16[4,128]{1,0:T(4,128)(2,1)} %bitcast.20, bf16[128,2048]{1,0:T(8,128)(2,1)} %tok_ref.1, bf16[128,2048]{1,0:T(8,128)(2,1)} %grad_ref.1), custom_call_target="tpu_custom_call" | custom-call | flops 1610612736 | bytes 7340032 | tf_op jit(solution)/shard_map/dispatch/pallas_call | solution.py:88
  6.1 86.8 %all_to_all.10 = bf16[128,8,3072]{2,1,0:T(8,128)(2,1)} all-to-all(bf16[128,8,3072]{2,1,0:T(8,128)(2,1)} %bitcast.22), channel_id=1, replica_groups=mesh['dp'=4,'expert'=32] {'dp','expert'}, dimensions={0} | all-to-all | bytes 12582912 | tf_op jit(solution)/shard_map/all_to_all | solution.py:269
  92.9 23.8 %middle.1 = (bf16[768,2048]{1,0:T(8,128)(2,1)}, bf16[768,2048]{1,0:T(8,128)(2,1)}, bf16[768,768]{1,0:T(8,128)(2,1)}, bf16[768,1536]{1,0:T(8,128)(2,1)}, bf16[1024,1664]{1,0:T(8,128)(2,1)}) custom-call(bf16[1024,3072]{1,0:T(8,128)(2,1)} %bitcast.23, bf16[2048,1536]{1,0:T(8,128)(2,1)} %bitcast.25, bf16[768,2048]{1,0:T(8,128)(2,1)} %bitcast.26), custom_call_target="tpu_custom_call" | custom-call | flops 16000000000 | bytes 29000000 | tf_op jit(solution)/shard_map/middle/pallas_call | solution.py:206
  116.7 4.7 %all-to-all-start.1 = ((bf16[128,8,1664]{2,1,0:T(8,128)(2,1)}), bf16[128,8,1664]{2,1,0:T(8,128)(2,1)S(1)}, u32[]{:S(2)}, u32[]{:S(2)}) async-start(bf16[128,8,1664]{2,1,0:T(8,128)(2,1)} %bitcast.24), calls=%async_computation.1 | async-start | bytes 6815744 | tf_op jit(solution)/shard_map/all_to_all | solution.py:269
  121.5 0.0 copy-start.2
  121.5 0.0 copy-start.3
  121.5 6.7 %fusion.1 = bf16[1,768,2048]{2,1,0:T(8,128)(2,1)} fusion(bf16[768,768]{1,0:T(8,128)(2,1)} %get-tuple-element.16, bf16[768,2048]{1,0:T(8,128)(2,1)} %get-tuple-element.17), kind=kOutput, calls=%fused_computation.3 | convolution fusion | flops 2417491968 | bytes 7471104 | tf_op jit(solution)/shard_map/dot_general | solution.py:30
  128.2 0.0 copy-done.2
  128.2 0.0 copy-done.3
  128.2 0.0 copy-start
  128.2 0.0 copy-start.1
  128.3 7.1 %fusion = bf16[1,2048,1536]{2,1,0:T(8,128)(2,1)} fusion(bf16[768,2048]{1,0:T(8,128)(2,1)S(1)} %copy-done.2, bf16[768,1536]{1,0:T(8,128)(2,1)S(1)} %copy-done.3), kind=kOutput, calls=%fused_computation.1 | convolution fusion | flops 4834983936 | bytes 11796480 | tf_op jit(solution)/shard_map/dot_general | solution.py:30
  135.3 30.5 %all-to-all-done.1 = bf16[128,8,1664]{2,1,0:T(8,128)(2,1)S(1)} async-done(((bf16[128,8,1664]{2,1,0:T(8,128)(2,1)}), bf16[128,8,1664]{2,1,0:T(8,128)(2,1)S(1)}, u32[]{:S(2)}, u32[]{:S(2)}) %all-to-all-start.1) | async-done | bytes 3407904 | tf_op jit(solution)/shard_map/all_to_all | solution.py:269
  165.9 0.0 copy-done
  165.9 0.0 copy-done.1
  165.9 2.3 %combine.1 = (bf16[128,2048]{1,0:T(8,128)(2,1)}, bf16[4,128]{1,0:T(4,128)(2,1)}) custom-call(s32[4,128]{1,0:T(4,128)S(1)} %bitcast.19, bf16[4,128]{1,0:T(4,128)(2,1)S(1)} %bitcast.21, bf16[1024,1664]{1,0:T(8,128)(2,1)S(1)} %bitcast.17), custom_call_target="tpu_custom_call" | custom-call | flops 805306368 | bytes 4000000 | tf_op jit(solution)/shard_map/combine/pallas_call | solution.py:257
Async XLA Ops:
  116.7 49.1 %all-to-all-start.1 = ((bf16[128,8,1664]{2,1,0:T(8,128)(2,1)}), bf16[128,8,1664]{2,1,0:T(8,128)(2,1)S(1)}, u32[]{:S(2)}, u32[]{:S(2)}) async-start(bf16[128,8,1664]{2,1,0:T(8,128)(2,1)} %bitcast.24), calls=%async_computation.1 | async-start | bytes 6815744 | tf_op jit(solution)/shard_map/all_to_all | solution.py:269
  121.5 6.7 %copy-start.2 = (bf16[768,2048]{1,0:T(8,128)(2,1)S(1)}, bf16[768,2048]{1,0:T(8,128)(2,1)}, u32[]{:S(2)}) copy-start(bf16[768,2048]{1,0:T(8,128)(2,1)} %get-tuple-element.14) | copy-start | bytes 9437188
  121.5 6.7 %copy-start.3 = (bf16[768,1536]{1,0:T(8,128)(2,1)S(1)}, bf16[768,1536]{1,0:T(8,128)(2,1)}, u32[]{:S(2)}) copy-start(bf16[768,1536]{1,0:T(8,128)(2,1)} %get-tuple-element.15) | copy-start | bytes 7077892
  128.2 37.6 %copy-start = (s32[128,4]{0,1:T(4,128)S(1)}, s32[128,4]{0,1:T(4,128)}, u32[]{:S(2)}) copy-start(s32[128,4]{0,1:T(4,128)} %param.8) | copy-start | bytes 6148
  128.2 37.6 %copy-start.1 = (bf16[128,4]{0,1:T(4,128)(2,1)S(1)}, bf16[128,4]{0,1:T(4,128)(2,1)}, u32[]{:S(2)}) copy-start(bf16[128,4]{0,1:T(4,128)(2,1)} %param.9) | copy-start | bytes 3076

commit v3 on v2

--- a/solution.py
+++ b/solution.py
@@ -145,30 +145,49 @@
             ref[here, MAIN:] = last.astype(BF16)
     out_x = pltpu.make_async_copy(x, x_hbm, out_sem.at[0])
     out_s = pltpu.make_async_copy(s, s_hbm, out_sem.at[1])
+    up_copy.wait()
+    down_copy.wait()
+    width, height = 256, 384
+    shares = [jnp.zeros((height, SUMS), F32) for _ in range(total // height)]
+
+    def finish(n, m, gate, lift, hid_grad):
+        here, at = slice(height * m, height * (m + 1)), width * n
+        sigma = 0.5 * jnp.tanh(0.5 * gate) + 0.5
+        gated = gate * sigma
+        derivative = sigma + gated * (1.0 - sigma)
+        hid = (gated * lift).astype(BF16)
+        hidden[here, at : at + width] = hid
+        pre_grad[here, at : at + width] = (hid_grad * lift * derivative).astype(BF16)
+        pre_grad[here, FF + at : FF + at + width] = (hid_grad * gated).astype(BF16)
+        share = hid.astype(F32) * hid_grad
+        for i in range(0, width, SUMS):
+            shares[m] = shares[m] + share[:, i : i + SUMS]
+
+    waiting = None
+    for n in range(FF // width):
+        at = width * n
+        for m in range(total // height):
+            here = slice(height * m, height * (m + 1))
+            made = (
+                n,
+                m,
+                dot(x[here, :], up[:, at : at + width]),
+                dot(x[here, :], up[:, FF + at : FF + at + width]),
+                dot_nt(s[here, :], down[at : at + width, :]),
+            )
+            if waiting is not None:
+                finish(*waiting)
+            waiting = made
+    finish(*waiting)
+    route = jnp.concatenate(shares, axis=0)
     out_x.start()
     out_s.start()
-    up_copy.wait()
-    down_copy.wait()
-    route = jnp.zeros((total, 1), F32)
-    width = 256
-    for n in range(FF // width):
-        at = width * n
-        gate = dot(x[...], up[:, at : at + width])
-        lift = dot(x[...], up[:, FF + at : FF + at + width])
-        hid_grad = dot_nt(s[...], down[at : at + width, :])
-        sigma = jax.nn.sigmoid(gate)
-        gated = gate * sigma
-        derivative = sigma * (1.0 + gate * (1.0 - sigma))
-        hid = (gated * lift).astype(BF16)
-        hidden[:, at : at + width] = hid
-        route = route + jnp.sum(hid.astype(F32) * hid_grad, axis=1, keepdims=True)
-        pre_grad[:, at : at + width] = (hid_grad * lift * derivative).astype(BF16)
-        pre_grad[:, FF + at : FF + at + width] = (hid_grad * gated).astype(BF16)
     out_h = pltpu.make_async_copy(hidden, hidden_hbm, out_sem.at[2])
     out_p = pltpu.make_async_copy(pre_grad, pre_grad_hbm, out_sem.at[3])
     out_h.start()
     out_p.start()
     put = [pack_match(rows, slots, 0, piece) for piece in (None, 0, 1, 2)]
+    route = jnp.sum(route, axis=1, keepdims=True)
     high = route.astype(BF16).astype(F32)
     lane = lax.broadcasted_iota(jnp.int32, (total, SUMS), 1)
     sums = jnp.where(lane == 0, high, jnp.where(lane == 1, route - high, 0.0)).astype(BF16)

time: 168 us -> 166 us (0.988)
  Pallas kernels: 31.6 us -> 29.2 us
    pallas_call x1, Pallas kernels: 23.8 us -> 21.4 us  [middle(): pl.pallas_call(middle_kernel, out_shape=shapes, in_specs=[hbm] * 3, out_s...]
where the time goes in v3:
time: 166 us
  blocking collectives  86.8 us (52%)
  waiting for transfers between devices  30.5 us (18%)
  Pallas kernels  29.2 us (18%)
  matrix products  13.8 us (8%)
  starting transfers between devices  4.75 us (3%)
    all_to_all x1, blocking collectives, exchange(): return lax.all_to_all(a, AXES, split_axis=0, concat_axis=0, tiled=True)  86.8 us
    all_to_all x1, waiting for transfers between devices, exchange(): return lax.all_to_all(a, AXES, split_axis=0, concat_axis=0, tiled=True)  30.5 us
    pallas_call x1, Pallas kernels, middle(): pl.pallas_call(middle_kernel, out_shape=shapes, in_specs=[hbm] * 3, out_s...  21.4 us
    dot_general x2, matrix products, dot_tn(): lax.dot_general(a, b, (((0,), (0,)), ((), ())), preferred_element_type=F32)  13.8 us
    pallas_call x1, Pallas kernels, dispatch(): pl.pallas_call(dispatch_kernel, grid=(TOK // GROUP,), out_shape=jax.Shape...  5.49 us
    all_to_all x1, starting transfers between devices, exchange(): return lax.all_to_all(a, AXES, split_axis=0, concat_axis=0, tiled=True)  4.75 us
  transfers between devices with their start and end apart: 1, of which 1 were waited for; matrix products, arithmetic and copies ran while one was open for 8% of the time, Pallas kernels for 0%

profile of v3, /device:TPU:1, one launch (start us, length us, event | category | flops | bytes accessed | tf_op | source)
XLA Modules:
  0.0 165.8 jit_solution(9788325342757587799)
XLA Ops:
  0.6 5.5 %dispatch.1 = bf16[1024,3072]{1,0:T(8,128)(2,1)} custom-call(s32[4,128]{1,0:T(4,128)} %bitcast.18, bf16[4,128]{1,0:T(4,128)(2,1)} %bitcast.20, bf16[128,2048]{1,0:T(8,128)(2,1)} %tok_ref.1, bf16[128,2048]{1,0:T(8,128)(2,1)} %grad_ref.1), custom_call_target="tpu_custom_call" | custom-call | flops 1610612736 | bytes 7340032 | tf_op jit(solution)/shard_map/dispatch/pallas_call | solution.py:88
  6.1 86.8 %all_to_all.10 = bf16[128,8,3072]{2,1,0:T(8,128)(2,1)} all-to-all(bf16[128,8,3072]{2,1,0:T(8,128)(2,1)} %bitcast.22), channel_id=1, replica_groups=mesh['dp'=4,'expert'=32] {'dp','expert'}, dimensions={0} | all-to-all | bytes 12582912 | tf_op jit(solution)/shard_map/all_to_all | solution.py:288
  92.9 21.4 %middle.1 = (bf16[768,2048]{1,0:T(8,128)(2,1)}, bf16[768,2048]{1,0:T(8,128)(2,1)}, bf16[768,768]{1,0:T(8,128)(2,1)}, bf16[768,1536]{1,0:T(8,128)(2,1)}, bf16[1024,1664]{1,0:T(8,128)(2,1)}) custom-call(bf16[1024,3072]{1,0:T(8,128)(2,1)} %bitcast.23, bf16[2048,1536]{1,0:T(8,128)(2,1)} %bitcast.25, bf16[768,2048]{1,0:T(8,128)(2,1)} %bitcast.26), custom_call_target="tpu_custom_call" | custom-call | flops 16000000000 | bytes 29000000 | tf_op jit(solution)/shard_map/middle/pallas_call | solution.py:225
  114.3 4.7 %all-to-all-start.1 = ((bf16[128,8,1664]{2,1,0:T(8,128)(2,1)}), bf16[128,8,1664]{2,1,0:T(8,128)(2,1)S(1)}, u32[]{:S(2)}, u32[]{:S(2)}) async-start(bf16[128,8,1664]{2,1,0:T(8,128)(2,1)} %bitcast.24), calls=%async_computation.1 | async-start | bytes 6815744 | tf_op jit(solution)/shard_map/all_to_all | solution.py:288
  119.1 0.0 copy-start.2
  119.1 0.0 copy-start.3
  119.1 6.7 %fusion.1 = bf16[1,768,2048]{2,1,0:T(8,128)(2,1)} fusion(bf16[768,768]{1,0:T(8,128)(2,1)} %get-tuple-element.16, bf16[768,2048]{1,0:T(8,128)(2,1)} %get-tuple-element.17), kind=kOutput, calls=%fused_computation.3 | convolution fusion | flops 2417491968 | bytes 7471104 | tf_op jit(solution)/shard_map/dot_general | solution.py:30
  125.8 0.0 copy-done.2
  125.8 0.0 copy-done.3
  125.8 0.0 copy-start
  125.8 0.0 copy-start.1
  125.8 7.1 %fusion = bf16[1,2048,1536]{2,1,0:T(8,128)(2,1)} fusion(bf16[768,2048]{1,0:T(8,128)(2,1)S(1)} %copy-done.2, bf16[768,1536]{1,0:T(8,128)(2,1)S(1)} %copy-done.3), kind=kOutput, calls=%fused_computation.1 | convolution fusion | flops 4834983936 | bytes 11796480 | tf_op jit(solution)/shard_map/dot_general | solution.py:30
  132.9 30.5 %all-to-all-done.1 = bf16[128,8,1664]{2,1,0:T(8,128)(2,1)S(1)} async-done(((bf16[128,8,1664]{2,1,0:T(8,128)(2,1)}), bf16[128,8,1664]{2,1,0:T(8,128)(2,1)S(1)}, u32[]{:S(2)}, u32[]{:S(2)}) %all-to-all-start.1) | async-done | bytes 3407904 | tf_op jit(solution)/shard_map/all_to_all | solution.py:288
  163.4 0.0 copy-done
  163.5 0.0 copy-done.1
  163.5 2.3 %combine.1 = (bf16[128,2048]{1,0:T(8,128)(2,1)}, bf16[4,128]{1,0:T(4,128)(2,1)}) custom-call(s32[4,128]{1,0:T(4,128)S(1)} %bitcast.19, bf16[4,128]{1,0:T(4,128)(2,1)S(1)} %bitcast.21, bf16[1024,1664]{1,0:T(8,128)(2,1)S(1)} %bitcast.17), custom_call_target="tpu_custom_call" | custom-call | flops 805306368 | bytes 4000000 | tf_op jit(solution)/shard_map/combine/pallas_call | solution.py:276
Async XLA Ops:
  114.3 49.1 %all-to-all-start.1 = ((bf16[128,8,1664]{2,1,0:T(8,128)(2,1)}), bf16[128,8,1664]{2,1,0:T(8,128)(2,1)S(1)}, u32[]{:S(2)}, u32[]{:S(2)}) async-start(bf16[128,8,1664]{2,1,0:T(8,128)(2,1)} %bitcast.24), calls=%async_computation.1 | async-start | bytes 6815744 | tf_op jit(solution)/shard_map/all_to_all | solution.py:288
  119.1 6.7 %copy-start.2 = (bf16[768,2048]{1,0:T(8,128)(2,1)S(1)}, bf16[768,2048]{1,0:T(8,128)(2,1)}, u32[]{:S(2)}) copy-start(bf16[768,2048]{1,0:T(8,128)(2,1)} %get-tuple-element.14) | copy-start | bytes 9437188
  119.1 6.7 %copy-start.3 = (bf16[768,1536]{1,0:T(8,128)(2,1)S(1)}, bf16[768,1536]{1,0:T(8,128)(2,1)}, u32[]{:S(2)}) copy-start(bf16[768,1536]{1,0:T(8,128)(2,1)} %get-tuple-element.15) | copy-start | bytes 7077892
  125.8 37.6 %copy-start = (s32[128,4]{0,1:T(4,128)S(1)}, s32[128,4]{0,1:T(4,128)}, u32[]{:S(2)}) copy-start(s32[128,4]{0,1:T(4,128)} %param.8) | copy-start | bytes 6148
  125.8 37.6 %copy-start.1 = (bf16[128,4]{0,1:T(4,128)(2,1)S(1)}, bf16[128,4]{0,1:T(4,128)(2,1)}, u32[]{:S(2)}) copy-start(bf16[128,4]{0,1:T(4,128)(2,1)} %param.9) | copy-start | bytes 3076

commit v4 on v3

--- a/solution.py
+++ b/solution.py
@@ -14,6 +14,7 @@
 PIECE = 512
 SUMS = 128
 GROUP = 32
+STEP = 16
 F32 = jnp.float32
 BF16 = jnp.bfloat16
 
@@ -68,12 +69,12 @@
                 rows_ref[a, j, :TOK, :] = ref[:, PIECE * j : PIECE * (j + 1)]
                 rows_ref[a, j, TOK:, :] = ref[:, MAIN:]
 
-    here = pl.ds(pl.multiple_of(step * GROUP, GROUP), GROUP)
+    here = pl.ds(pl.multiple_of(step * STEP, STEP), STEP)
     pos = spread(pos_ref[here, :])
     weight = spread(weight_ref[here, :])
-    main = pos == slot_of_row(GROUP * 8, None)
+    main = pos == slot_of_row(STEP * 8, None)
     for j in range(3):
-        part = pos == slot_of_row(GROUP * 8, j)
+        part = pos == slot_of_row(STEP * 8, j)
         for a in range(2):
             value = 1.0 if a == 0 else weight
             pick = jnp.concatenate(
@@ -87,10 +88,10 @@
     whole = lambda shape: pl.BlockSpec(shape, lambda i: (0, 0))
     return pl.pallas_call(
         dispatch_kernel,
-        grid=(TOK // GROUP,),
+        grid=(TOK // STEP,),
         out_shape=jax.ShapeDtypeStruct((TOK * 8, 2 * MAIN), BF16),
         in_specs=[whole(ids.shape), whole(w.shape), whole(tokens.shape), whole(grads.shape)],
-        out_specs=pl.BlockSpec((GROUP * 8, 2 * MAIN), lambda i: (i, 0)),
+        out_specs=pl.BlockSpec((STEP * 8, 2 * MAIN), lambda i: (i, 0)),
         scratch_shapes=[
             pltpu.VMEM((TOK, TOK), F32),
             pltpu.VMEM((TOK, TOK), F32),

time: 166 us -> 167 us (level)
  no operation moved by 1% of the time
where the time goes in v4:
time: 167 us
  blocking collectives  86.8 us (52%)
  Pallas kernels  30.6 us (18%)
  waiting for transfers between devices  30.5 us (18%)
  matrix products  13.8 us (8%)
  starting transfers between devices  4.75 us (3%)
    all_to_all x1, blocking collectives, exchange(): return lax.all_to_all(a, AXES, split_axis=0, concat_axis=0, tiled=True)  86.8 us
    all_to_all x1, waiting for transfers between devices, exchange(): return lax.all_to_all(a, AXES, split_axis=0, concat_axis=0, tiled=True)  30.5 us
    pallas_call x1, Pallas kernels, middle(): pl.pallas_call(middle_kernel, out_shape=shapes, in_specs=[hbm] * 3, out_s...  21.4 us
    dot_general x2, matrix products, dot_tn(): lax.dot_general(a, b, (((0,), (0,)), ((), ())), preferred_element_type=F32)  13.8 us
    pallas_call x1, Pallas kernels, dispatch(): pl.pallas_call(dispatch_kernel, grid=(TOK // STEP,), out_shape=jax.ShapeD...  6.89 us
    all_to_all x1, starting transfers between devices, exchange(): return lax.all_to_all(a, AXES, split_axis=0, concat_axis=0, tiled=True)  4.75 us
  transfers between devices with their start and end apart: 1, of which 1 were waited for; matrix products, arithmetic and copies ran while one was open for 8% of the time, Pallas kernels for 0%

profile of v4, /device:TPU:1, one launch (start us, length us, event | category | flops | bytes accessed | tf_op | source)
XLA Modules:
  0.0 167.1 jit_solution(17413780603614686564)
XLA Ops:
  0.6 6.9 %dispatch.1 = bf16[1024,3072]{1,0:T(8,128)(2,1)} custom-call(s32[4,128]{1,0:T(4,128)} %bitcast.18, bf16[4,128]{1,0:T(4,128)(2,1)} %bitcast.20, bf16[128,2048]{1,0:T(8,128)(2,1)} %tok_ref.1, bf16[128,2048]{1,0:T(8,128)(2,1)} %grad_ref.1), custom_call_target="tpu_custom_call" | custom-call | flops 1610612736 | bytes 7340032 | tf_op jit(solution)/shard_map/dispatch/pallas_call | solution.py:89
  7.5 86.8 %all_to_all.10 = bf16[128,8,3072]{2,1,0:T(8,128)(2,1)} all-to-all(bf16[128,8,3072]{2,1,0:T(8,128)(2,1)} %bitcast.22), channel_id=1, replica_groups=mesh['dp'=4,'expert'=32] {'dp','expert'}, dimensions={0} | all-to-all | bytes 12582912 | tf_op jit(solution)/shard_map/all_to_all | solution.py:289
  94.3 21.4 %middle.1 = (bf16[768,2048]{1,0:T(8,128)(2,1)}, bf16[768,2048]{1,0:T(8,128)(2,1)}, bf16[768,768]{1,0:T(8,128)(2,1)}, bf16[768,1536]{1,0:T(8,128)(2,1)}, bf16[1024,1664]{1,0:T(8,128)(2,1)}) custom-call(bf16[1024,3072]{1,0:T(8,128)(2,1)} %bitcast.23, bf16[2048,1536]{1,0:T(8,128)(2,1)} %bitcast.25, bf16[768,2048]{1,0:T(8,128)(2,1)} %bitcast.26), custom_call_target="tpu_custom_call" | custom-call | flops 16000000000 | bytes 29000000 | tf_op jit(solution)/shard_map/middle/pallas_call | solution.py:226
  115.7 4.7 %all-to-all-start.1 = ((bf16[128,8,1664]{2,1,0:T(8,128)(2,1)}), bf16[128,8,1664]{2,1,0:T(8,128)(2,1)S(1)}, u32[]{:S(2)}, u32[]{:S(2)}) async-start(bf16[128,8,1664]{2,1,0:T(8,128)(2,1)} %bitcast.24), calls=%async_computation.1 | async-start | bytes 6815744 | tf_op jit(solution)/shard_map/all_to_all | solution.py:289
  120.5 0.0 copy-start.2
  120.5 0.0 copy-start.3
  120.5 6.7 %fusion.1 = bf16[1,768,2048]{2,1,0:T(8,128)(2,1)} fusion(bf16[768,768]{1,0:T(8,128)(2,1)} %get-tuple-element.16, bf16[768,2048]{1,0:T(8,128)(2,1)} %get-tuple-element.17), kind=kOutput, calls=%fused_computation.3 | convolution fusion | flops 2417491968 | bytes 7471104 | tf_op jit(solution)/shard_map/dot_general | solution.py:31
  127.2 0.0 copy-done.2
  127.2 0.0 copy-done.3
  127.2 0.0 copy-start
  127.2 0.0 copy-start.1
  127.2 7.1 %fusion = bf16[1,2048,1536]{2,1,0:T(8,128)(2,1)} fusion(bf16[768,2048]{1,0:T(8,128)(2,1)S(1)} %copy-done.2, bf16[768,1536]{1,0:T(8,128)(2,1)S(1)} %copy-done.3), kind=kOutput, calls=%fused_computation.1 | convolution fusion | flops 4834983936 | bytes 11796480 | tf_op jit(solution)/shard_map/dot_general | solution.py:31
  134.3 30.5 %all-to-all-done.1 = bf16[128,8,1664]{2,1,0:T(8,128)(2,1)S(1)} async-done(((bf16[128,8,1664]{2,1,0:T(8,128)(2,1)}), bf16[128,8,1664]{2,1,0:T(8,128)(2,1)S(1)}, u32[]{:S(2)}, u32[]{:S(2)}) %all-to-all-start.1) | async-done | bytes 3407904 | tf_op jit(solution)/shard_map/all_to_all | solution.py:289
  164.8 0.0 copy-done
  164.8 0.0 copy-done.1
  164.8 2.3 %combine.1 = (bf16[128,2048]{1,0:T(8,128)(2,1)}, bf16[4,128]{1,0:T(4,128)(2,1)}) custom-call(s32[4,128]{1,0:T(4,128)S(1)} %bitcast.19, bf16[4,128]{1,0:T(4,128)(2,1)S(1)} %bitcast.21, bf16[1024,1664]{1,0:T(8,128)(2,1)S(1)} %bitcast.17), custom_call_target="tpu_custom_call" | custom-call | flops 805306368 | bytes 4000000 | tf_op jit(solution)/shard_map/combine/pallas_call | solution.py:277
Async XLA Ops:
  115.7 49.1 %all-to-all-start.1 = ((bf16[128,8,1664]{2,1,0:T(8,128)(2,1)}), bf16[128,8,1664]{2,1,0:T(8,128)(2,1)S(1)}, u32[]{:S(2)}, u32[]{:S(2)}) async-start(bf16[128,8,1664]{2,1,0:T(8,128)(2,1)} %bitcast.24), calls=%async_computation.1 | async-start | bytes 6815744 | tf_op jit(solution)/shard_map/all_to_all | solution.py:289
  120.5 6.7 %copy-start.2 = (bf16[768,2048]{1,0:T(8,128)(2,1)S(1)}, bf16[768,2048]{1,0:T(8,128)(2,1)}, u32[]{:S(2)}) copy-start(bf16[768,2048]{1,0:T(8,128)(2,1)} %get-tuple-element.14) | copy-start | bytes 9437188
  120.5 6.7 %copy-start.3 = (bf16[768,1536]{1,0:T(8,128)(2,1)S(1)}, bf16[768,1536]{1,0:T(8,128)(2,1)}, u32[]{:S(2)}) copy-start(bf16[768,1536]{1,0:T(8,128)(2,1)} %get-tuple-element.15) | copy-start | bytes 7077892
  127.2 37.6 %copy-start = (s32[128,4]{0,1:T(4,128)S(1)}, s32[128,4]{0,1:T(4,128)}, u32[]{:S(2)}) copy-start(s32[128,4]{0,1:T(4,128)} %param.8) | copy-start | bytes 6148
  127.2 37.6 %copy-start.1 = (bf16[128,4]{0,1:T(4,128)(2,1)S(1)}, bf16[128,4]{0,1:T(4,128)(2,1)}, u32[]{:S(2)}) copy-start(bf16[128,4]{0,1:T(4,128)(2,1)} %param.9) | copy-start | bytes 3076
